TPU v7x, 512 devices: a whole 4x4x16 slice. The times are simulated.
512 devices in a mesh: ctx: 64 (over y, z), ch: 8 (over x, core).
Axes of the slice: x: 4, y: 4, z: 16, core: 2. Of those that a mesh axis runs over, the one named last changes fastest.
Arguments:
- query_rows: bfloat16 [8192, 8192], P('ctx', 'ch'), may hold values from -6 to 6
- key_rows: bfloat16 [8192, 8192], P('ctx', 'ch'), may hold values from -6 to 6
- value_rows: bfloat16 [8192, 8192], P('ctx', 'ch'), may hold values from -6 to 6
- short_filter: float32 [3, 3, 8192], P(None, None, 'ch'), may hold values from -3.5 to 3.5
- decay_rate: float32 [8192, 16], P('ch'), may hold values from 2e-05 to 0.1
- residues: float32 [8192, 16], P('ch'), may hold values from -1.5 to 1.5
- out_weight: bfloat16 [8192, 4096], P('ctx', 'ch'), may hold values from -0.1875 to 0.1875
- record_starts: int32 [4], replicated, may hold values from 0 to 8191, as said below
Outputs:
- block_out: bfloat16 [8192, 4096], P('ctx', 'ch')
Inputs may be any that keep to these rules, and one draw needn't show every extreme that they name: record_starts[0] is 0 and the last entry is 8191; the entries are distinct and increasing, and all but the first lie in the second half of the 8192 tokens.
All inputs are finite; a program needn't handle non-finite values.
Results may differ from a plain program's by a relative error of at most 0.017.
Values may be sent and summed in bfloat16 or wider, within the bound.
A program may use at most 64 MiB of HBM per device.

v0:
```python
import jax
import jax.numpy as jnp
from jax import lax
from jax.sharding import PartitionSpec as P

MODES = 16
KS = 3


def shifted(block, axis, distance):
    devices = range(lax.axis_size(axis))
    route = [(i - distance, i) for i in devices if i - distance in devices]
    return lax.ppermute(block, axis, route)


def carried_in(x, axis, combine, identity):
    devices, mine = (lax.axis_size(axis), lax.axis_index(axis))
    everything = jax.tree.map(lambda part: lax.all_gather(part, axis), x)
    start = jax.tree.map(
        lambda part, zero: jnp.broadcast_to(jnp.asarray(zero, part.dtype), part.shape), x, identity
    )

    def hop(k, before):
        reached = k < mine
        new = combine(before, jax.tree.map(lambda part: part[k], everything))
        return jax.tree.map(lambda a, b: jnp.where(reached, a, b), new, before)

    return lax.fori_loop(0, devices, hop, start)


def ages_of(positions, record_starts):
    earlier = record_starts[None, :] <= positions[:, None]
    segment = jnp.max(jnp.where(earlier, record_starts[None, :], 0), axis=1)
    return positions - segment


def masked_conv(extended, weights, ages, count):
    taps = weights.shape[0]
    total = jnp.zeros((count, extended.shape[1]), jnp.float32)
    for tap_index in range(taps):
        keeper = (ages >= tap_index).astype(jnp.float32)[:, None]
        window = extended[taps - 1 - tap_index : taps - 1 - tap_index + count]
        total = total + weights[tap_index][None, :] * window * keeper
    return total


def combine_pairs(earlier, later_pair):
    return (earlier[0] * later_pair[0], later_pair[0] * earlier[1] + later_pair[1])


def local(
    query_rows, key_rows, value_rows, short_filter, decay_rate, residues, out_weight, record_starts
):
    row_count, channels = query_rows.shape
    anchor = lax.axis_index("ctx") * row_count
    positions = anchor + jnp.arange(row_count, dtype=jnp.int32)
    ages = ages_of(positions, record_starts)
    reach_short = KS - 1
    tails = shifted(
        (
            query_rows[row_count - reach_short :],
            key_rows[row_count - reach_short :],
            value_rows[row_count - reach_short :],
        ),
        "ctx",
        1,
    )
    query_conv = masked_conv(
        jnp.concatenate([tails[0], query_rows], axis=0).astype(jnp.float32),
        short_filter[0],
        ages,
        row_count,
    )
    key_conv = masked_conv(
        jnp.concatenate([tails[1], key_rows], axis=0).astype(jnp.float32),
        short_filter[1],
        ages,
        row_count,
    )
    value_conv = masked_conv(
        jnp.concatenate([tails[2], value_rows], axis=0).astype(jnp.float32),
        short_filter[2],
        ages,
        row_count,
    )
    mixed = (key_conv * value_conv).astype(jnp.bfloat16).astype(jnp.float32)
    gain = jnp.sqrt(1.0 - jnp.exp(-2.0 * decay_rate))
    block_rows = 8
    block_count = row_count // block_rows
    inner_index = jnp.arange(block_rows, dtype=jnp.float32)
    inner_ints = jnp.arange(block_rows, dtype=jnp.int32)
    rising = jnp.exp(-decay_rate[None, :, :] * inner_index[:, None, None])
    taps_inner = jnp.sum(rising * (residues * gain)[None, :, :], axis=2)
    local_index = jnp.arange(row_count, dtype=jnp.int32)
    inner_ages = jnp.minimum(ages, local_index % block_rows)
    padded_mixed = jnp.concatenate(
        [jnp.zeros((block_rows - 1, channels), jnp.float32), mixed], axis=0
    )
    within = masked_conv(padded_mixed, taps_inner, inner_ages, row_count)
    entry_powers = jnp.exp(-decay_rate[None, :, :] * (inner_index[:, None, None] + 1.0))
    final_powers = (
        jnp.exp(-decay_rate[None, :, :] * (block_rows - 1.0 - inner_index[:, None, None]))
        * gain[None, :, :]
    )
    block_decay = jnp.exp(-decay_rate * block_rows)
    mixed_blocks = mixed.reshape(block_count, block_rows, channels)
    age_blocks = ages.reshape(block_count, block_rows)
    last_ages = age_blocks[:, block_rows - 1]
    weighted = (last_ages[:, None] >= block_rows - 1 - inner_ints[None, :]).astype(jnp.float32)
    endings = jnp.einsum("rcm,brc->bcm", final_powers, mixed_blocks * weighted[:, :, None])
    unbroken = (last_ages >= block_rows).astype(jnp.float32)

    def advance(state, inputs):
        ending, kept = inputs
        return (block_decay * kept * state + ending, state)

    local_state, entering_states = lax.scan(
        advance, jnp.zeros((channels, MODES), jnp.float32), (endings, unbroken)
    )
    entering = (age_blocks > inner_ints[None, :]).astype(jnp.float32)
    between = (
        jnp.einsum("rcm,bcm->brc", entry_powers, residues[None, :, :] * entering_states)
        * entering[:, :, None]
    )
    device_decay = jnp.exp(-decay_rate * row_count) * (ages[row_count - 1] >= row_count).astype(
        jnp.float32
    )
    identity_pair = (jnp.ones_like(device_decay), jnp.zeros_like(local_state))
    carried = carried_in((device_decay, local_state), "ctx", combine_pairs, identity_pair)[1]
    block_index = jnp.arange(block_count, dtype=jnp.float32)
    block_starts = jnp.exp(-decay_rate[None, :, :] * (block_index[:, None, None] * block_rows))
    coefficient = block_starts * (residues * carried)[None, :, :]
    correction = jnp.einsum("rcm,bcm->brc", entry_powers, coefficient).reshape(row_count, channels)
    untouched = (ages > local_index).astype(jnp.float32)[:, None]
    filtered = within + between.reshape(row_count, channels) + correction * untouched
    gated = (query_conv * filtered).astype(jnp.bfloat16)
    all_channels = lax.all_gather(gated, "ch", axis=1, tiled=True)
    result = jnp.dot(
        all_channels,
        lax.all_gather(out_weight, "ctx", axis=0, tiled=True),
        preferred_element_type=jnp.float32,
    )
    return result.astype(jnp.bfloat16)


def solution(mesh):
    return jax.shard_map(
        local,
        mesh=mesh,
        in_specs=(
            P("ctx", "ch"),
            P("ctx", "ch"),
            P("ctx", "ch"),
            P(None, None, "ch"),
            P("ch", None),
            P("ch", None),
            P("ctx", "ch"),
            P(),
        ),
        out_specs=P("ctx", "ch"),
        check_vma=False,
    )
```

profile of v0, /device:TPU:2, one launch (start us, length us, event | category | flops | bytes accessed | tf_op | source)
XLA Modules:
  0.0 616.6 jit_solution(5873278730106274515)
XLA Ops:
  7.3 3.8 collective-permute-start.1
  11.8 3.8 collective-permute-start.2
  17.6 1.6 fusion.59
  23.6 2.8 copy.59
  26.3 5.7 fusion.16
  32.1 5.2 copy.61
  37.3 32.3 %while.27 = (s32[]{:T(128)}, f32[1024,16]{0,1:T(8,128)S(1)}, f32[16,1024,16]{1,2,0:T(8,128)}, f32[16]{0:T(128)S(1)}, f32[1024,16]{0,1:T(8,128)S(1)}, /*index=5*/f32[16,1024,16]{1,2,0:T(8,128)S(1)}, s32[]{:T(128)}, s32[]{:T(128)}) while((s32[]{:T(128)}, f32[1024,16]{0,1:T(8,128)S(1)}, f32[16,1024,16]{1,2,0:T(8,128)}, ...), condition=%wide.region_3.4_spmd.clone, body=%wide.region_2.3_spmd.clone.sunk | while | flops 81923 | bytes 393844 | solution.py:117
  70.3 3.8 collective-permute-start
  75.6 2.1 slice_reduce_fusion.7
  77.9 4.9 copy.62
  82.8 6.5 %multiply_bitcast_fusion = f32[16,8,1024]{0,1,2:T(8,128)} fusion(bf16[16,1024,16]{2,0,1:T(8,128)(2,1)} %copy.62, f32[16,8]{0,1:T(8,128)S(1)} %copy.63, f32[8]{0:T(128)S(1)} %iota_add_fusion, f32[1024,16]{1,0:T(8,128)S(1)} %copy.57), kind=kOutput, calls=%fused_computation.16 | convolution fusion | flops 4456448 | bytes 1114656 | tf_op jit(solution)/shard_map/rcm,bcm->brc/dot_general | solution.py:122
  89.3 3.0 copy.64
  92.3 76.4 %all-gather.11.cloned.1.call-done = f32[65536,16]{0,1:T(8,128)} async-done(((f32[1024,16]{0,1:T(8,128)}), f32[65536,16]{0,1:T(8,128)}) %all-gather.11.cloned.1.call-update) | async-done | bytes 4194320 | tf_op jit(solution)/shard_map/all_gather | solution.py:18
  168.7 6.5 %copy.72 = f32[2,8,64,1024]{3,2,1,0:T(8,128)} copy(f32[2,8,64,1024]{3,1,2,0:T(8,128)} %bitcast.68) | data formatting | bytes 8388608
  175.3 137.7 %all-gather.13.cloned.1.call-done = f32[65536,16]{0,1:T(8,128)} async-done(((f32[1024,16]{0,1:T(8,128)}), f32[65536,16]{0,1:T(8,128)}) %all-gather.13.cloned.1.call-update) | async-done | bytes 4194320 | tf_op jit(solution)/shard_map/all_gather | solution.py:18
  313.0 6.6 %copy.73 = f32[2,8,64,1024]{3,2,1,0:T(8,128)} copy(f32[2,8,64,1024]{3,1,2,0:T(8,128)} %bitcast.69) | data formatting | bytes 8388608
  319.6 88.1 %while.28 = (s32[]{:T(128)}, f32[1024,16]{0,1:T(8,128)S(1)}, s32[]{:T(128)}, f32[64,1024,16]{1,0,2:T(8,128)}, f32[64,1024,16]{1,0,2:T(8,128)}, /*index=5*/s32[]{:T(128)}, s32[]{:T(128)}) while((s32[]{:T(128)}, f32[1024,16]{0,1:T(8,128)S(1)}, s32[]{:T(128)}, f32[64,1024,16]{1,0,2:T(8,128)}, f32[64,1024,16]{1,0,2:T(8,128)}, ...), condition=%wide.region_5.6_spmd.clone, body=%wide.region_4.5_spmd.clone.sunk | while | flops 65540 | bytes 524389 | solution.py:28
  322.3 1.3 constant_dynamic-slice_fusion.3
  323.7 1.3 constant_dynamic-slice_fusion.3
  325.1 1.3 constant_dynamic-slice_fusion.3
  326.4 1.3 constant_dynamic-slice_fusion.3
  327.8 1.3 constant_dynamic-slice_fusion.3
  329.2 1.3 constant_dynamic-slice_fusion.3
  330.6 1.3 constant_dynamic-slice_fusion.3
  332.0 1.3 constant_dynamic-slice_fusion.3
  333.3 1.3 constant_dynamic-slice_fusion.3
  407.9 3.9 fusion.21
  411.7 3.0 copy.69
  414.7 1.7 fusion.47
  417.0 26.1 %all-gather.7.cloned.1.call-done = bf16[128,8192]{1,0:T(8,128)(2,1)} async-done(((bf16[128,1024]{1,0:T(8,128)(2,1)}), bf16[128,8192]{1,0:T(8,128)(2,1)}) %all-gather.7.cloned.1.call-update) | async-done | bytes 2097168 | tf_op jit(solution)/shard_map/all_gather | solution.py:137
  443.1 161.0 %all-gather.9.cloned.1.call-done = bf16[8192,512]{1,0:T(8,128)(2,1)} async-done(((bf16[128,512]{1,0:T(8,128)(2,1)}), bf16[8192,512]{1,0:T(8,128)(2,1)}) %all-gather.9.cloned.1.call-update) | async-done | bytes 8388624 | tf_op jit(solution)/shard_map/all_gather | solution.py:140
  604.1 5.9 convolution_convert_fusion
  (219 shorter events, 116.6 us)
Async XLA Ops:
  6.5 162.2 %all-gather.11.cloned.1.call-start = ((), (), s32[]{:S(2)}) async-start(), calls=%async_computation.2 | async-start | bytes 4259840 | tf_op jit(solution)/shard_map/all_gather | solution.py:18
  7.3 13.7 %collective-permute-start.1 = (bf16[2,1024]{1,0:T(2,128)(2,1)S(1)}, bf16[2,1024]{1,0:T(2,128)(2,1)S(1)}, u32[]{:S(2)}, u32[]{:S(2)}) collective-permute-start(bf16[2,1024]{1,0:T(2,128)(2,1)S(1)} %slice.146), channel_id=1, source_target_pairs={{0,8},{8,16},{16,24},{24,32},{32,40},{40,48},{48,56},{56,64},{64,7... | collective-permute-start | bytes 12296 | tf_op jit(solution)/shard_map/ppermute | solution.py:13
  11.8 10.2 %collective-permute-start.2 = (bf16[2,1024]{1,0:T(2,128)(2,1)S(1)}, bf16[2,1024]{1,0:T(2,128)(2,1)S(1)}, u32[]{:S(2)}, u32[]{:S(2)}) collective-permute-start(bf16[2,1024]{1,0:T(2,128)(2,1)S(1)} %slice.153), channel_id=1, source_target_pairs={{0,8},{8,16},{16,24},{24,32},{32,40},{40,48},{48,56},{56,64},{64,7... | collective-permute-start | bytes 12296 | tf_op jit(solution)/shard_map/ppermute | solution.py:13
  19.2 293.8 %all-gather.13.cloned.1.call-start = ((), (), s32[]{:S(2)}) async-start(), calls=%async_computation.3 | async-start | bytes 4259840 | tf_op jit(solution)/shard_map/all_gather | solution.py:18
  32.1 38.2 %copy-start.3 = (bf16[128,1024]{1,0:T(8,128)(2,1)S(1)}, bf16[128,1024]{1,0:T(8,128)(2,1)}, u32[]{:S(2)}) copy-start(bf16[128,1024]{1,0:T(8,128)(2,1)} %param.12) | copy-start | bytes 786436
  37.3 40.5 %copy-start.2 = (f32[1024,16]{0,1:T(8,128)S(1)}, f32[1024,16]{0,1:T(8,128)}, u32[]{:S(2)}) copy-start(f32[1024,16]{0,1:T(8,128)} %param.17) | copy-start | bytes 196612
  69.6 0.6 copy-start
  69.6 8.2 %copy-start.1 = (f32[16,1024,16]{1,2,0:T(8,128)S(1)}, f32[16,1024,16]{1,2,0:T(8,128)}, u32[]{:S(2)}) copy-start(f32[16,1024,16]{1,2,0:T(8,128)} %get-tuple-element.132) | copy-start | bytes 3145732
  70.2 372.9 %all-gather.7.cloned.1.call-start = ((), (), s32[]{:S(2)}) async-start(), calls=%async_computation | async-start | bytes 2359296 | tf_op jit(solution)/shard_map/all_gather | solution.py:137
  70.3 22.0 %collective-permute-start = (bf16[2,1024]{1,0:T(2,128)(2,1)S(1)}, bf16[2,1024]{1,0:T(2,128)(2,1)S(1)}, u32[]{:S(2)}, u32[]{:S(2)}) collective-permute-start(bf16[2,1024]{1,0:T(2,128)(2,1)S(1)} %slice.138), channel_id=1, source_target_pairs={{0,8},{8,16},{16,24},{24,32},{32,40},{40,48},{48,56},{56,64},{64,7... | collective-permute-start | bytes 12296 | tf_op jit(solution)/shard_map/ppermute | solution.py:13
  416.5 187.7 %all-gather.9.cloned.1.call-start = ((), (), s32[]{:S(2)}) async-start(), calls=%async_computation.1 | async-start | bytes 8519680 | tf_op jit(solution)/shard_map/all_gather | solution.py:140
Sparse Core Ops, SparseCore 0:
  19.3 149.3 all-gather.10
  171.7 141.2 all-gather.12
  416.6 26.4 all-gather.6
  445.9 158.1 all-gather.8
where the time goes:
time: 619 us; the launch traced here: 617 us
  waiting for transfers between devices  402 us (65%)
  local copies, waits for them, and re-layouts  133 us (21%)
  other arithmetic  32.3 us (5%)
  matrix products  22.1 us (4%)
  between operations  14.1 us (2%)
  starting transfers between devices  11.6 us (2%)
    all_gather x2, waiting for transfers between devices, carried_in(): everything = jax.tree.map(lambda part: lax.all_gather(part, axis), x)  214 us
    all_gather x1, waiting for transfers between devices, local(): lax.all_gather(out_weight, 'ctx', axis=0, tiled=True)  161 us
    dynamic_slice x64, local copies, waits for them, and re-layouts, hop(): new = combine(before, jax.tree.map(lambda part: part[k], everything))  83.4 us
    all_gather x1, waiting for transfers between devices, local(): all_channels = lax.all_gather(gated, 'ch', axis=1, tiled=True)  26.1 us
    unnamed x11, local copies, waits for them, and re-layouts  18.9 us
  transfers between devices with their start and end apart: 7, of which 4 were waited for; matrix products, arithmetic and copies ran while one was open for 13% of the time, Pallas kernels for 0%

commit v1 on v0

v1 whole, which is shorter than its diff:
```python
import functools

import jax
import jax.numpy as jnp
from jax import lax
from jax.experimental import pallas as pl
from jax.experimental.pallas import tpu as pltpu
from jax.sharding import PartitionSpec as P

MODES = 16
KS = 3
NX, NY, NZ, NC = 4, 4, 16, 2
TOK = 128
CH = 1024
G = CH // 128
COLS = 512
HALF = TOK // 2
MESH = pl.DeviceIdType.MESH
F32 = jnp.float32
BF16 = jnp.bfloat16


def exp_small(r):
    out = jnp.full_like(r, 1.0 / 5040.0)
    for c in (1.0 / 720.0, 1.0 / 120.0, 1.0 / 24.0, 1.0 / 6.0, 0.5, 1.0):
        out = c - r * out
    return 1.0 - r * out


def one_minus_exp(u):
    out = jnp.full_like(u, 1.0 / 40320.0)
    for c in (1.0 / 5040.0, 1.0 / 720.0, 1.0 / 120.0, 1.0 / 24.0, 1.0 / 6.0, 0.5, 1.0):
        out = c - u * out
    return u * out


def tree(parts):
    while len(parts) > 1:
        parts = [
            parts[i] + parts[i + 1] if i + 1 < len(parts) else parts[i]
            for i in range(0, len(parts), 2)
        ]
    return parts[0]


def kernel(
    q_in, k_in, v_in, sf_in, rate_in, res_in, w_in, rs,
    out_ref,
    q_raw, k_raw, v_raw, qt, kt, vt, xt, yt, gt, sft, ratet, rest, lamt, wt,
    fin, got, ebuf, rbuf, rgot, gref, ent, wbuf, abuf, pbuf, qbuf, rsum,
    load_sem, halo_send, halo_recv, tr_sem, wsend, wrecv,
    s1_send, s1_recv, s2_send, s2_recv, s3_send, s3_recv,
    a_send, a_recv, sib_send, sib_recv, c_send, c_recv, x_send, x_recv,
):
    ctx = lax.axis_index("ctx")
    ch = lax.axis_index("ch")
    y, z = ctx // NZ, lax.rem(ctx, NZ)
    x, c = ch // NC, lax.rem(ch, NC)

    def dev(xx, cc, yy, zz):
        return (yy * NZ + zz, xx * NC + cc)

    def zpeer(d):
        return lax.rem(z + d, NZ)

    def ypeer(d):
        return lax.rem(y + d, NY)

    def xpeer(d):
        return lax.rem(x + d, NX)

    n_ctx = NY * NZ
    after = (lax.rem(ctx + 1, n_ctx), ch)
    before = (lax.rem(ctx + n_ctx - 1, n_ctx), ch)
    sibling = dev(x, 1 - c, y, z)
    flipped = dev(y, c, x, z)

    barrier = pltpu.get_barrier_semaphore()

    def greet(d):
        pl.semaphore_signal(barrier, inc=1, device_id=d, device_id_type=MESH)

    for d in range(1, NZ):
        greet(dev(x, c, y, zpeer(d)))
    for d in range(1, NY):
        greet(dev(x, c, ypeer(d), z))
    for d in range(1, NX):
        greet(dev(xpeer(d), c, y, z))
    greet(sibling)
    greet(before)
    greet(after)

    @pl.when(x != y)
    def _():
        greet(flipped)

    loads = [
        pltpu.make_async_copy(src, dst, load_sem.at[i])
        for i, (src, dst) in enumerate(((k_in, k_raw), (v_in, v_raw), (q_in, q_raw)))
    ]
    for load in loads:
        load.start()

    for g in range(G):
        lanes = slice(g * 128, (g + 1) * 128)
        ratet[pl.ds(g, MODES, stride=G), :] = rate_in[:, lanes]
        rest[pl.ds(g, MODES, stride=G), :] = res_in[:, lanes]
        for i in range(3):
            sft[pl.ds(i * KS * G + g, KS, stride=G), :] = sf_in[i, :, lanes]
    rate_all = ratet[...]
    lamt[...] = exp_small(rate_all)
    wt[...] = rest[...] * jnp.sqrt(one_minus_exp(2.0 * rate_all))

    def spread(raw, dst):
        for g in range(G):
            lanes = slice(g * 128, (g + 1) * 128)
            dst[pl.ds(2 * G + g, TOK, stride=G), :] = raw[:, lanes].astype(F32)

    loads[0].wait()
    spread(k_raw, kt)
    loads[1].wait()
    spread(v_raw, vt)
    loads[2].wait()
    spread(q_raw, qt)

    partners = (NZ - 1) + (NY - 1) + (NX - 1) + 3 + jnp.where(x != y, 1, 0)
    pl.semaphore_wait(barrier, partners)

    halos = []
    for i, arr in enumerate((kt, vt, qt)):
        halos.append(
            pltpu.make_async_remote_copy(
                src_ref=arr.at[pl.ds(TOK * G, 2 * G), :],
                dst_ref=arr.at[pl.ds(0, 2 * G), :],
                send_sem=halo_send.at[i],
                recv_sem=halo_recv.at[i],
                device_id=after,
                device_id_type=MESH,
            )
        )

    def wslot(s):
        return wbuf.at[pl.ds(pl.multiple_of(s * TOK, TOK), TOK), :]

    def wpart(s, first, count):
        return wbuf.at[pl.ds(pl.multiple_of(s * TOK + first, HALF), count), :]

    flip = pltpu.make_async_remote_copy(
        src_ref=w_in,
        dst_ref=wslot(z),
        send_sem=tr_sem.at[0],
        recv_sem=tr_sem.at[1],
        device_id=flipped,
        device_id_type=MESH,
    )
    keep_w = pltpu.make_async_copy(w_in, wslot(z), tr_sem.at[2])

    @pl.when(x != y)
    def _():
        flip.start()

    @pl.when(x == y)
    def _():
        keep_w.start()

    for h in halos:
        h.start()

    def wcopy(s, right):
        first, count = 0, TOK
        if s == NZ // 2 - 1:
            first, count = (0, HALF) if right else (HALF, HALF)
        slot = lax.rem(z + NZ - s, NZ) if right else lax.rem(z + s, NZ)
        side = 0 if right else 1
        return pltpu.make_async_remote_copy(
            src_ref=wpart(slot, first, count),
            dst_ref=wpart(slot, first, count),
            send_sem=wsend.at[side, s],
            recv_sem=wrecv.at[side, s],
            device_id=dev(x, c, y, zpeer(1 if right else NZ - 1)),
            device_id_type=MESH,
        )

    def w_step(s):
        if s == 0:
            @pl.when(x != y)
            def _():
                flip.wait_recv()

            @pl.when(x == y)
            def _():
                keep_w.wait()
        else:
            wcopy(s - 1, True).wait_recv()
            wcopy(s - 1, False).wait_recv()
        if s < NZ // 2:
            wcopy(s, True).start()
            wcopy(s, False).start()

    base = ctx * TOK
    starts = [rs[i] for i in range(4)]

    def seg_of(pos):
        seg = jnp.int32(0)
        for st in starts:
            seg = jnp.maximum(seg, jnp.where(st <= pos, st, 0))
        return seg

    def tile(ref, t):
        return ref[pl.ds(pl.multiple_of(t * G, G), G), :]

    def put(ref, t, val):
        ref[pl.ds(pl.multiple_of(t * G, G), G), :] = val

    def age_masks(pos):
        age = pos - seg_of(pos)
        return jnp.where(age >= 1, 1.0, 0.0).astype(F32), jnp.where(age >= 2, 1.0, 0.0).astype(F32)

    def taps(i):
        return [sft[(i * KS + j) * G : (i * KS + j + 1) * G, :] for j in range(KS)]

    def conv(ref, w, t, m1, m2):
        return w[0] * tile(ref, t + 2) + w[1] * tile(ref, t + 1) * m1 + w[2] * tile(ref, t) * m2

    def mix(t):
        m1, m2 = age_masks(base + t)
        return (conv(kt, taps(1), t, m1, m2) * conv(vt, taps(2), t, m1, m2)).astype(BF16).astype(F32)

    lams = lambda: [lamt[m * G : (m + 1) * G, :] for m in range(MODES)]
    ws = lambda: [wt[m * G : (m + 1) * G, :] for m in range(MODES)]
    last_seg = seg_of(base + TOK - 1)

    def pass1(i, state):
        lam = lams()
        for u in range(6):
            t = 2 + i * 6 + u
            val = mix(t)
            put(xt, t, val)
            val = val * jnp.where(base + t >= last_seg, 1.0, 0.0).astype(F32)
            state = [s * l + val for s, l in zip(state, lam)]
        return state

    zero = jnp.zeros((G, 128), F32)
    state = lax.fori_loop(0, (TOK - 2) // 6, pass1, [zero] * MODES)
    w_step(0)
    halos[0].wait_recv()
    halos[1].wait_recv()
    val0, val1 = mix(0), mix(1)
    put(xt, 0, val0)
    put(xt, 1, val1)
    val0 = val0 * jnp.where(base >= last_seg, 1.0, 0.0).astype(F32)
    val1 = val1 * jnp.where(base + 1 >= last_seg, 1.0, 0.0).astype(F32)
    for m in range(MODES):
        rows = slice(m * G, (m + 1) * G)
        far = jnp.exp(ratet[rows, :] * (-(TOK - 2.0)))
        fin[rows, :] = state[m] + far * (lamt[rows, :] * val0 + val1)

    def zexchange(src, dst, send, recv):
        def one(d):
            peer = zpeer(d)
            return pltpu.make_async_remote_copy(
                src_ref=src.at[pl.ds(pl.multiple_of(peer * G, G), G), :],
                dst_ref=dst.at[pl.ds(pl.multiple_of(z * G, G), G), :],
                send_sem=send.at[d],
                recv_sem=recv.at[d],
                device_id=dev(x, c, y, peer),
                device_id_type=MESH,
            )

        return [one(d) for d in range(1, NZ)]

    to_mode = zexchange(fin, got, s1_send, s1_recv)
    for cp in to_mode:
        cp.start()
    put(got, z, tile(fin, z))

    halos[2].wait_recv()

    def qconv(i, carry):
        for u in range(8):
            t = i * 8 + u
            m1, m2 = age_masks(base + t)
            put(gt, t, conv(qt, taps(0), t, m1, m2))
        return carry

    def local_part(i, state):
        lam, w = lams(), ws()
        for u in range(8):
            t = i * 8 + u
            val = tile(xt, t)
            m1, _ = age_masks(base + t)
            state = [s * m1 * l + val for s, l in zip(state, lam)]
            put(yt, t, tree([a * b for a, b in zip(w, state)]))
        return state

    lax.fori_loop(0, TOK // 8, qconv, 0)
    w_step(1)
    state = lax.fori_loop(0, TOK // 16, local_part, [zero] * MODES)

    def unbroken(first, count):
        hit = jnp.int32(0)
        for st in starts:
            hit = hit + jnp.where((st >= first) & (st < first + count), 1, 0)
        return jnp.where(hit == 0, 1.0, 0.0).astype(F32)

    for cp in to_mode:
        cp.wait_recv()
    rate_m = tile(ratet, z)
    one_block = jnp.exp(rate_m * (-float(TOK)))
    one_row = jnp.exp(rate_m * (-float(TOK * NZ)))
    entry = zero
    for zz in range(NZ):
        ebuf[zz * G : (zz + 1) * G, :] = entry
        entry = entry * (one_block * unbroken((y * NZ + zz) * TOK, TOK)) + got[zz * G : (zz + 1) * G, :]
    rbuf[...] = entry

    to_rows = [
        pltpu.make_async_remote_copy(
            src_ref=rbuf,
            dst_ref=rgot.at[pl.ds(pl.multiple_of(y * G, G), G), :],
            send_sem=s2_send.at[d],
            recv_sem=s2_recv.at[d],
            device_id=dev(x, c, ypeer(d), z),
            device_id_type=MESH,
        )
        for d in range(1, NY)
    ]
    for cp in to_rows:
        cp.start()
    state = lax.fori_loop(TOK // 16, TOK // 8, local_part, state)
    w_step(2)
    for cp in to_rows:
        cp.wait_recv()
    gref[...] = zero
    for yy in range(NY - 1):
        @pl.when(yy < y)
        def _():
            gref[...] = gref[...] * (one_row * unbroken(yy * NZ * TOK, NZ * TOK)) + rgot[yy * G : (yy + 1) * G, :]

    entry = gref[...]
    for zz in range(NZ):
        rows = slice(zz * G, (zz + 1) * G)
        ebuf[rows, :] = ebuf[rows, :] + entry
        entry = entry * (one_block * unbroken((y * NZ + zz) * TOK, TOK))
    to_back = zexchange(ebuf, ent, s3_send, s3_recv)
    for cp in to_back:
        cp.start()
    put(ent, z, tile(ebuf, z))
    for cp in to_back:
        cp.wait_recv()

    def correct(i, state):
        lam = lams()
        for u in range(8):
            t = i * 8 + u
            free = jnp.where(seg_of(base + t) < base, 1.0, 0.0).astype(F32)
            filtered = tile(yt, t) + tree(list(state)) * free
            put(gt, t, tile(gt, t) * filtered)
            state = [s * l for s, l in zip(state, lam)]
        return state

    init = []
    for m in range(MODES):
        rows = slice(m * G, (m + 1) * G)
        init.append(ent[rows, :] * lamt[rows, :] * wt[rows, :])
    state = init

    def ablock(yy, cc, h):
        return abuf.at[yy, cc, pl.ds(h * HALF, HALF), :]

    def acopy(yy, h, right, index):
        return pltpu.make_async_remote_copy(
            src_ref=ablock(yy, c, h),
            dst_ref=ablock(yy, c, h),
            send_sem=a_send.at[index],
            recv_sem=a_recv.at[index],
            device_id=dev(x, c, ypeer(1 if right else NY - 1), z),
            device_id_type=MESH,
        )

    def sibcopy(d, h):
        yy = ypeer(d)
        return pltpu.make_async_remote_copy(
            src_ref=ablock(yy, c, h),
            dst_ref=ablock(yy, c, h),
            send_sem=sib_send.at[d, h],
            recv_sem=sib_recv.at[d, h],
            device_id=sibling,
            device_id_type=MESH,
        )

    for h in range(2):
        state = lax.fori_loop(h * (TOK // 16), (h + 1) * (TOK // 16), correct, state)
        for g in range(G):
            part = gt[pl.ds(h * HALF * G + g, HALF, stride=G), :].astype(BF16)
            abuf[y, c, h * HALF : (h + 1) * HALF, g * 128 : (g + 1) * 128] = part
        acopy(y, h, True, h).start()
        acopy(y, h, False, 2 + h).start()
        sibcopy(0, h).start()

    w_step(3)
    left, right, far = ypeer(NY - 1), ypeer(1), ypeer(2)
    acopy(y, 0, True, 0).wait_recv()
    acopy(left, 0, True, 4).start()
    sibcopy(3, 0).start()
    acopy(y, 0, False, 2).wait_recv()
    sibcopy(1, 0).start()
    w_step(4)
    acopy(y, 1, False, 3).wait_recv()
    acopy(right, 1, False, 5).start()
    sibcopy(1, 1).start()
    acopy(y, 1, True, 1).wait_recv()
    sibcopy(3, 1).start()
    w_step(5)
    acopy(far, 0, True, 4).wait_recv()
    sibcopy(2, 0).start()
    w_step(6)
    acopy(far, 1, False, 5).wait_recv()
    sibcopy(2, 1).start()
    w_step(7)
    w_step(8)

    def product(yy):
        acc = jnp.dot(abuf[yy, 0], wbuf[0:CH, :], preferred_element_type=F32)
        return acc + jnp.dot(abuf[yy, 1], wbuf[CH : 2 * CH, :], preferred_element_type=F32)

    def ccopy(d):
        return pltpu.make_async_remote_copy(
            src_ref=pbuf.at[d],
            dst_ref=qbuf.at[y],
            send_sem=c_send.at[d],
            recv_sem=c_recv.at[d],
            device_id=dev(x, c, ypeer(d), z),
            device_id_type=MESH,
        )

    def xcopy(o, d):
        return pltpu.make_async_remote_copy(
            src_ref=qbuf.at[o],
            dst_ref=rsum.at[x],
            send_sem=x_send.at[d],
            recv_sem=x_recv.at[d],
            device_id=dev(o, c, y, z),
            device_id_type=MESH,
        )

    def pass_on(o):
        for d in range(1, NX):
            @pl.when(o == xpeer(d))
            def _():
                xcopy(xpeer(d), d).start()

        @pl.when(o == x)
        def _():
            rsum[x] = qbuf[o]

    for d in (2, 1, 3, 0):
        for h in range(2):
            sibcopy(d, h).wait_recv()
        res = product(ypeer(d)).astype(BF16)
        if d == 0:
            qbuf[y] = res
            pass_on(y)
        else:
            pbuf[d] = res
            ccopy(d).start()
    for d in (3, 1, 2):
        ccopy(d).wait_recv()
        pass_on(ypeer(NY - d))
    for d in range(1, NX):
        xcopy(xpeer(d), d).wait_recv()
    total = rsum[0].astype(F32) + rsum[1].astype(F32) + rsum[2].astype(F32) + rsum[3].astype(F32)
    out_ref[...] = total.astype(BF16)

    @pl.when(x != y)
    def _():
        flip.wait_send()

    for h in halos:
        h.wait_send()
    for s in range(NZ // 2):
        wcopy(s, True).wait_send()
        wcopy(s, False).wait_send()
    for cp in to_mode + to_rows + to_back:
        cp.wait_send()
    for h in range(2):
        acopy(y, h, True, h).wait_send()
        acopy(y, h, False, 2 + h).wait_send()
    acopy(left, 0, True, 4).wait_send()
    acopy(right, 1, False, 5).wait_send()
    for d in range(NY):
        for h in range(2):
            sibcopy(d, h).wait_send()
    for d in range(1, NY):
        ccopy(d).wait_send()
    for d in range(1, NX):
        xcopy(xpeer(d), d).wait_send()


def local(
    query_rows, key_rows, value_rows, short_filter, decay_rate, residues, out_weight, record_starts
):
    vmem = pl.BlockSpec(memory_space=pltpu.VMEM)
    hbm = pl.BlockSpec(memory_space=pl.ANY)
    smem = pl.BlockSpec(memory_space=pltpu.SMEM)
    tokens = pltpu.VMEM((TOK * G, 128), F32)
    longer = pltpu.VMEM(((TOK + 2) * G, 128), F32)
    table = pltpu.VMEM((MODES * G, 128), F32)
    dma = pltpu.SemaphoreType.DMA
    return pl.pallas_call(
        kernel,
        out_shape=jax.ShapeDtypeStruct((TOK, COLS), BF16),
        in_specs=[hbm, hbm, hbm, vmem, vmem, vmem, hbm, smem],
        out_specs=vmem,
        scratch_shapes=[
            pltpu.VMEM((TOK, CH), BF16), pltpu.VMEM((TOK, CH), BF16), pltpu.VMEM((TOK, CH), BF16),
            longer, longer, longer, tokens, tokens, tokens,
            pltpu.VMEM((9 * G, 128), F32), table, table, table, table,
            table, table, table, pltpu.VMEM((G, 128), F32), pltpu.VMEM((NY * G, 128), F32),
            pltpu.VMEM((G, 128), F32), table,
            pltpu.VMEM((NZ * TOK, COLS), BF16),
            pltpu.VMEM((NY, NC, TOK, CH), BF16),
            pltpu.VMEM((NY, TOK, COLS), BF16),
            pltpu.VMEM((NY, TOK, COLS), BF16),
            pltpu.VMEM((NX, TOK, COLS), BF16),
            dma((3,)), dma((3,)), dma((3,)), dma((3,)), dma((2, 8)), dma((2, 8)),
            dma((NZ,)), dma((NZ,)), dma((NY,)), dma((NY,)), dma((NZ,)), dma((NZ,)),
            dma((6,)), dma((6,)), dma((NY, 2)), dma((NY, 2)),
            dma((NY,)), dma((NY,)), dma((NX,)), dma((NX,)),
        ],
        compiler_params=pltpu.CompilerParams(
            collective_id=0, has_side_effects=True, vmem_limit_bytes=40 * 1024 * 1024
        ),
    )(
        query_rows, key_rows, value_rows, short_filter,
        decay_rate.T, residues.T, out_weight, record_starts,
    )


def solution(mesh):
    return jax.shard_map(
        local,
        mesh=mesh,
        in_specs=(
            P("ctx", "ch"),
            P("ctx", "ch"),
            P("ctx", "ch"),
            P(None, None, "ch"),
            P("ch", None),
            P("ch", None),
            P("ctx", "ch"),
            P(),
        ),
        out_specs=P("ctx", "ch"),
        check_vma=False,
    )
```

time: 619 us -> 95 us (0.15)
  the two profiles are of different devices: /device:TPU:2 before, /device:TPU:16 now
where the time goes in v1:
time: 95 us; the launch traced here: 94.6 us
  Pallas kernels  87 us (92%)
  local copies, waits for them, and re-layouts  7.54 us (8%)
    pallas_call x1, Pallas kernels, local(): pl.pallas_call(kernel, out_shape=jax.ShapeDtypeStruct((TOK, COLS), BF16),...  87 us
    unnamed x17, local copies, waits for them, and re-layouts  7.54 us

profile of v1, /device:TPU:16, one launch (start us, length us, event | category | flops | bytes accessed | tf_op | source)
XLA Modules:
  0.0 94.6 jit_solution(8296614155185403484)
XLA Ops:
  0.0 0.0 copy-start.7
  0.0 0.7 copy-done.7
  0.7 0.0 copy-start
  0.7 0.9 %copy-done = bf16[128,1024]{1,0:T(8,128)(2,1)S(1)} copy-done((bf16[128,1024]{1,0:T(8,128)(2,1)S(1)}, bf16[128,1024]{1,0:T(8,128)(2,1)}, u32[]{:S(2)}) %copy-start) | copy-done | bytes 262168
  1.6 0.0 copy-start.1
  1.6 0.9 %copy-done.1 = bf16[128,1024]{1,0:T(8,128)(2,1)S(1)} copy-done((bf16[128,1024]{1,0:T(8,128)(2,1)S(1)}, bf16[128,1024]{1,0:T(8,128)(2,1)}, u32[]{:S(2)}) %copy-start.1) | copy-done | bytes 262168
  2.6 0.0 copy-start.2
  2.6 0.9 %copy-done.2 = bf16[128,1024]{1,0:T(8,128)(2,1)S(1)} copy-done((bf16[128,1024]{1,0:T(8,128)(2,1)S(1)}, bf16[128,1024]{1,0:T(8,128)(2,1)}, u32[]{:S(2)}) %copy-start.2) | copy-done | bytes 262168
  3.5 0.0 copy-start.3
  3.5 0.9 copy-done.3
  4.4 0.0 copy-start.4
  4.4 0.8 copy-done.4
  5.3 0.0 copy-start.5
  5.3 0.8 copy-done.5
  6.1 0.0 copy-start.6
  6.1 0.8 copy-done.6
  6.9 87.0 %shard_map.82 = bf16[128,512]{1,0:T(8,128)(2,1)S(1)} custom-call(bf16[128,1024]{1,0:T(8,128)(2,1)S(1)} %copy-done, bf16[128,1024]{1,0:T(8,128)(2,1)S(1)} %copy-done.1, bf16[128,1024]{1,0:T(8,128)(2,1)S(1)} %copy-done.2, f32[3,3,1024]{2,1,0:T(4,128)S(1)} %copy-done.6, f32[16,1024]{1,0:T(8,128)S(1)} %bitcast.2, f32[16,1024]{1,0:T(8,128)S(1)} %bitcast.3, ...), custom_call_target="tpu_custom_call" | custom-call | tf_op jit(solution)/shard_map/pallas_call | solution.py:510
  93.9 0.7 copy.10
Async XLA Ops:
  0.0 0.7 copy-start.7
  0.7 0.9 %copy-start = (bf16[128,1024]{1,0:T(8,128)(2,1)S(1)}, bf16[128,1024]{1,0:T(8,128)(2,1)}, u32[]{:S(2)}) copy-start(bf16[128,1024]{1,0:T(8,128)(2,1)} %q_in.1) | copy-start | bytes 786436
  1.6 0.9 %copy-start.1 = (bf16[128,1024]{1,0:T(8,128)(2,1)S(1)}, bf16[128,1024]{1,0:T(8,128)(2,1)}, u32[]{:S(2)}) copy-start(bf16[128,1024]{1,0:T(8,128)(2,1)} %k_in.1) | copy-start | bytes 786436
  2.6 0.9 %copy-start.2 = (bf16[128,1024]{1,0:T(8,128)(2,1)S(1)}, bf16[128,1024]{1,0:T(8,128)(2,1)}, u32[]{:S(2)}) copy-start(bf16[128,1024]{1,0:T(8,128)(2,1)} %v_in.1) | copy-start | bytes 786436
  3.5 0.9 copy-start.3
  4.4 0.8 copy-start.4
  5.3 0.8 copy-start.5
  6.1 0.8 copy-start.6

commit v2 on v1

--- a/solution.py
+++ b/solution.py
@@ -15,6 +15,8 @@
 G = CH // 128
 COLS = 512
 HALF = TOK // 2
+PIECES = 4
+PIECE = TOK // PIECES
 MESH = pl.DeviceIdType.MESH
 F32 = jnp.float32
 BF16 = jnp.bfloat16
@@ -44,11 +46,11 @@
 
 
 def kernel(
-    q_in, k_in, v_in, sf_in, rate_in, res_in, w_in, rs,
+    q_in, k_in, v_in, sf_hbm, rate_hbm, res_hbm, w_in, rs,
     out_ref,
-    q_raw, k_raw, v_raw, qt, kt, vt, xt, yt, gt, sft, ratet, rest, lamt, wt,
+    q_raw, k_raw, v_raw, sf_in, rate_in, res_in, qt, kt, vt, xt, yt, gt, sft, ratet, rest, lamt, wt,
     fin, got, ebuf, rbuf, rgot, gref, ent, wbuf, abuf, pbuf, qbuf, rsum,
-    load_sem, halo_send, halo_recv, tr_sem, wsend, wrecv,
+    load_sem, halo_send, halo_recv, tr_sem, keep_sem, wsend, wrecv,
     s1_send, s1_recv, s2_send, s2_recv, s3_send, s3_recv,
     a_send, a_recv, sib_send, sib_recv, c_send, c_recv, x_send, x_recv,
 ):
@@ -74,6 +76,18 @@
     before = (lax.rem(ctx + n_ctx - 1, n_ctx), ch)
     sibling = dev(x, 1 - c, y, z)
     flipped = dev(y, c, x, z)
+
+    loads = [
+        pltpu.make_async_copy(src, dst, load_sem.at[i])
+        for i, (src, dst) in enumerate(
+            (
+                (k_in, k_raw), (v_in, v_raw), (q_in, q_raw),
+                (rate_hbm, rate_in), (res_hbm, res_in), (sf_hbm, sf_in),
+            )
+        )
+    ]
+    for load in loads:
+        load.start()
 
     barrier = pltpu.get_barrier_semaphore()
 
@@ -93,35 +107,6 @@
     @pl.when(x != y)
     def _():
         greet(flipped)
-
-    loads = [
-        pltpu.make_async_copy(src, dst, load_sem.at[i])
-        for i, (src, dst) in enumerate(((k_in, k_raw), (v_in, v_raw), (q_in, q_raw)))
-    ]
-    for load in loads:
-        load.start()
-
-    for g in range(G):
-        lanes = slice(g * 128, (g + 1) * 128)
-        ratet[pl.ds(g, MODES, stride=G), :] = rate_in[:, lanes]
-        rest[pl.ds(g, MODES, stride=G), :] = res_in[:, lanes]
-        for i in range(3):
-            sft[pl.ds(i * KS * G + g, KS, stride=G), :] = sf_in[i, :, lanes]
-    rate_all = ratet[...]
-    lamt[...] = exp_small(rate_all)
-    wt[...] = rest[...] * jnp.sqrt(one_minus_exp(2.0 * rate_all))
-
-    def spread(raw, dst):
-        for g in range(G):
-            lanes = slice(g * 128, (g + 1) * 128)
-            dst[pl.ds(2 * G + g, TOK, stride=G), :] = raw[:, lanes].astype(F32)
-
-    loads[0].wait()
-    spread(k_raw, kt)
-    loads[1].wait()
-    spread(v_raw, vt)
-    loads[2].wait()
-    spread(q_raw, qt)
 
     partners = (NZ - 1) + (NY - 1) + (NX - 1) + 3 + jnp.where(x != y, 1, 0)
     pl.semaphore_wait(barrier, partners)
@@ -143,59 +128,96 @@
         return wbuf.at[pl.ds(pl.multiple_of(s * TOK, TOK), TOK), :]
 
     def wpart(s, first, count):
-        return wbuf.at[pl.ds(pl.multiple_of(s * TOK + first, HALF), count), :]
-
-    flip = pltpu.make_async_remote_copy(
-        src_ref=w_in,
-        dst_ref=wslot(z),
-        send_sem=tr_sem.at[0],
-        recv_sem=tr_sem.at[1],
-        device_id=flipped,
-        device_id_type=MESH,
-    )
-    keep_w = pltpu.make_async_copy(w_in, wslot(z), tr_sem.at[2])
+        return wbuf.at[pl.ds(pl.multiple_of(s * TOK + first, PIECE), count), :]
+
+    def flip(k):
+        return pltpu.make_async_remote_copy(
+            src_ref=w_in.at[pl.ds(k * PIECE, PIECE), :],
+            dst_ref=wpart(z, k * PIECE, PIECE),
+            send_sem=tr_sem.at[0, k],
+            recv_sem=tr_sem.at[1, k],
+            device_id=flipped,
+            device_id_type=MESH,
+        )
+
+    keep_w = pltpu.make_async_copy(w_in, wslot(z), keep_sem.at[0])
 
     @pl.when(x != y)
     def _():
-        flip.start()
+        for k in range(PIECES):
+            flip(k).start()
 
     @pl.when(x == y)
     def _():
         keep_w.start()
 
-    for h in halos:
-        h.start()
-
-    def wcopy(s, right):
-        first, count = 0, TOK
-        if s == NZ // 2 - 1:
-            first, count = (0, HALF) if right else (HALF, HALF)
-        slot = lax.rem(z + NZ - s, NZ) if right else lax.rem(z + s, NZ)
+    def spread(raw, dst, first, count):
+        for g in range(G):
+            lanes = slice(g * 128, (g + 1) * 128)
+            dst[pl.ds((2 + first) * G + g, count, stride=G), :] = raw[first : first + count, lanes].astype(F32)
+
+    for i, (raw, dst) in enumerate(((k_raw, kt), (v_raw, vt))):
+        loads[i].wait()
+        spread(raw, dst, TOK - 16, 16)
+        halos[i].start()
+
+    for load in loads[3:]:
+        load.wait()
+    for g in range(G):
+        lanes = slice(g * 128, (g + 1) * 128)
+        ratet[pl.ds(g, MODES, stride=G), :] = rate_in[:, lanes]
+        rest[pl.ds(g, MODES, stride=G), :] = res_in[:, lanes]
+        for i in range(3):
+            sft[pl.ds(i * KS * G + g, KS, stride=G), :] = sf_in[i, :, lanes]
+    rate_all = ratet[...]
+    lamt[...] = exp_small(rate_all)
+    wt[...] = rest[...] * jnp.sqrt(one_minus_exp(2.0 * rate_all))
+
+    spread(k_raw, kt, 0, TOK - 16)
+    spread(v_raw, vt, 0, TOK - 16)
+    loads[2].wait()
+    spread(q_raw, qt, TOK - 16, 16)
+    halos[2].start()
+    spread(q_raw, qt, 0, TOK - 16)
+
+    STEPS = NZ // 2
+
+    def wcopy(n, right):
+        hop, part = n // PIECES, n % PIECES
+        slot = lax.rem(z + NZ - hop, NZ) if right else lax.rem(z + hop, NZ)
         side = 0 if right else 1
         return pltpu.make_async_remote_copy(
-            src_ref=wpart(slot, first, count),
-            dst_ref=wpart(slot, first, count),
-            send_sem=wsend.at[side, s],
-            recv_sem=wrecv.at[side, s],
+            src_ref=wpart(slot, part * PIECE, PIECE),
+            dst_ref=wpart(slot, part * PIECE, PIECE),
+            send_sem=wsend.at[side, n],
+            recv_sem=wrecv.at[side, n],
             device_id=dev(x, c, y, zpeer(1 if right else NZ - 1)),
             device_id_type=MESH,
         )
 
-    def w_step(s):
-        if s == 0:
+    def w_goes(n, right):
+        return n < PIECES * STEPS and (n // PIECES < STEPS - 1 or (n % 2 == 0) == right)
+
+    def w_step(n):
+        if n < PIECES:
             @pl.when(x != y)
             def _():
-                flip.wait_recv()
-
-            @pl.when(x == y)
-            def _():
-                keep_w.wait()
-        else:
-            wcopy(s - 1, True).wait_recv()
-            wcopy(s - 1, False).wait_recv()
-        if s < NZ // 2:
-            wcopy(s, True).start()
-            wcopy(s, False).start()
+                flip(n).wait_recv()
+
+            if n == 0:
+                @pl.when(x == y)
+                def _():
+                    keep_w.wait()
+
+        for right in (True, False):
+            if n >= PIECES and w_goes(n - PIECES, right):
+                wcopy(n - PIECES, right).wait_recv()
+            if w_goes(n, right):
+                wcopy(n, right).start()
+
+    def w_hop(h):
+        for part in range(PIECES):
+            w_step(h * PIECES + part)
 
     base = ctx * TOK
     starts = [rs[i] for i in range(4)]
@@ -242,7 +264,6 @@
 
     zero = jnp.zeros((G, 128), F32)
     state = lax.fori_loop(0, (TOK - 2) // 6, pass1, [zero] * MODES)
-    w_step(0)
     halos[0].wait_recv()
     halos[1].wait_recv()
     val0, val1 = mix(0), mix(1)
@@ -294,8 +315,10 @@
         return state
 
     lax.fori_loop(0, TOK // 8, qconv, 0)
-    w_step(1)
     state = lax.fori_loop(0, TOK // 16, local_part, [zero] * MODES)
+    w_hop(0)
+    state = lax.fori_loop(TOK // 16, TOK // 8, local_part, state)
+    w_hop(1)
 
     def unbroken(first, count):
         hit = jnp.int32(0)
@@ -327,8 +350,7 @@
     ]
     for cp in to_rows:
         cp.start()
-    state = lax.fori_loop(TOK // 16, TOK // 8, local_part, state)
-    w_step(2)
+    w_hop(2)
     for cp in to_rows:
         cp.wait_recv()
     gref[...] = zero
@@ -346,6 +368,8 @@
     for cp in to_back:
         cp.start()
     put(ent, z, tile(ebuf, z))
+    for hop in (3, 4, 5):
+        w_hop(hop)
     for cp in to_back:
         cp.wait_recv()
 
@@ -394,31 +418,26 @@
         for g in range(G):
             part = gt[pl.ds(h * HALF * G + g, HALF, stride=G), :].astype(BF16)
             abuf[y, c, h * HALF : (h + 1) * HALF, g * 128 : (g + 1) * 128] = part
+        if h == 1:
+            acopy(y, 1, False, 3).start()
         acopy(y, h, True, h).start()
-        acopy(y, h, False, 2 + h).start()
         sibcopy(0, h).start()
-
-    w_step(3)
-    left, right, far = ypeer(NY - 1), ypeer(1), ypeer(2)
+    acopy(y, 0, False, 2).start()
+
+    lhs, rhs, far = ypeer(NY - 1), ypeer(1), ypeer(2)
+    w_hop(6)
     acopy(y, 0, True, 0).wait_recv()
-    acopy(left, 0, True, 4).start()
+    acopy(lhs, 0, True, 4).start()
     sibcopy(3, 0).start()
+    acopy(y, 1, False, 3).wait_recv()
+    acopy(rhs, 1, False, 5).start()
+    sibcopy(1, 1).start()
+    w_hop(7)
+    acopy(y, 1, True, 1).wait_recv()
+    sibcopy(3, 1).start()
     acopy(y, 0, False, 2).wait_recv()
     sibcopy(1, 0).start()
-    w_step(4)
-    acopy(y, 1, False, 3).wait_recv()
-    acopy(right, 1, False, 5).start()
-    sibcopy(1, 1).start()
-    acopy(y, 1, True, 1).wait_recv()
-    sibcopy(3, 1).start()
-    w_step(5)
-    acopy(far, 0, True, 4).wait_recv()
-    sibcopy(2, 0).start()
-    w_step(6)
-    acopy(far, 1, False, 5).wait_recv()
-    sibcopy(2, 1).start()
-    w_step(7)
-    w_step(8)
+    w_hop(8)
 
     def product(yy):
         acc = jnp.dot(abuf[yy, 0], wbuf[0:CH, :], preferred_element_type=F32)
@@ -454,16 +473,25 @@
         def _():
             rsum[x] = qbuf[o]
 
-    for d in (2, 1, 3, 0):
+    def send_product(d):
         for h in range(2):
             sibcopy(d, h).wait_recv()
-        res = product(ypeer(d)).astype(BF16)
+        part = product(ypeer(d)).astype(BF16)
         if d == 0:
-            qbuf[y] = res
+            qbuf[y] = part
             pass_on(y)
         else:
-            pbuf[d] = res
+            pbuf[d] = part
             ccopy(d).start()
+
+    send_product(3)
+    send_product(1)
+    acopy(far, 0, True, 4).wait_recv()
+    sibcopy(2, 0).start()
+    acopy(far, 1, False, 5).wait_recv()
+    sibcopy(2, 1).start()
+    send_product(0)
+    send_product(2)
     for d in (3, 1, 2):
         ccopy(d).wait_recv()
         pass_on(ypeer(NY - d))
@@ -474,20 +502,22 @@
 
     @pl.when(x != y)
     def _():
-        flip.wait_send()
+        for k in range(PIECES):
+            flip(k).wait_send()
 
     for h in halos:
         h.wait_send()
-    for s in range(NZ // 2):
-        wcopy(s, True).wait_send()
-        wcopy(s, False).wait_send()
+    for n in range(PIECES * STEPS):
+        for right in (True, False):
+            if w_goes(n, right):
+                wcopy(n, right).wait_send()
     for cp in to_mode + to_rows + to_back:
         cp.wait_send()
     for h in range(2):
         acopy(y, h, True, h).wait_send()
         acopy(y, h, False, 2 + h).wait_send()
-    acopy(left, 0, True, 4).wait_send()
-    acopy(right, 1, False, 5).wait_send()
+    acopy(lhs, 0, True, 4).wait_send()
+    acopy(rhs, 1, False, 5).wait_send()
     for d in range(NY):
         for h in range(2):
             sibcopy(d, h).wait_send()
@@ -510,10 +540,11 @@
     return pl.pallas_call(
         kernel,
         out_shape=jax.ShapeDtypeStruct((TOK, COLS), BF16),
-        in_specs=[hbm, hbm, hbm, vmem, vmem, vmem, hbm, smem],
+        in_specs=[hbm] * 7 + [smem],
         out_specs=vmem,
         scratch_shapes=[
             pltpu.VMEM((TOK, CH), BF16), pltpu.VMEM((TOK, CH), BF16), pltpu.VMEM((TOK, CH), BF16),
+            pltpu.VMEM((3, KS, CH), F32), pltpu.VMEM((MODES, CH), F32), pltpu.VMEM((MODES, CH), F32),
             longer, longer, longer, tokens, tokens, tokens,
             pltpu.VMEM((9 * G, 128), F32), table, table, table, table,
             table, table, table, pltpu.VMEM((G, 128), F32), pltpu.VMEM((NY * G, 128), F32),
@@ -523,13 +554,13 @@
             pltpu.VMEM((NY, TOK, COLS), BF16),
             pltpu.VMEM((NY, TOK, COLS), BF16),
             pltpu.VMEM((NX, TOK, COLS), BF16),
-            dma((3,)), dma((3,)), dma((3,)), dma((3,)), dma((2, 8)), dma((2, 8)),
+            dma((6,)), dma((3,)), dma((3,)), dma((2, PIECES)), dma((1,)), dma((2, 32)), dma((2, 32)),
             dma((NZ,)), dma((NZ,)), dma((NY,)), dma((NY,)), dma((NZ,)), dma((NZ,)),
             dma((6,)), dma((6,)), dma((NY, 2)), dma((NY, 2)),
             dma((NY,)), dma((NY,)), dma((NX,)), dma((NX,)),
         ],
         compiler_params=pltpu.CompilerParams(
-            collective_id=0, has_side_effects=True, vmem_limit_bytes=40 * 1024 * 1024
+            collective_id=0, has_side_effects=True, vmem_limit_bytes=60 * 1024 * 1024
         ),
     )(
         query_rows, key_rows, value_rows, short_filter,

time: 95 us -> 74.6 us (0.79)
  Pallas kernels: 87 us -> 72.7 us
  local copies, waits for them, and re-layouts: 7.54 us -> 1.57 us
    pallas_call x1, Pallas kernels: 87 us -> 72.7 us  [local(): pl.pallas_call(kernel, out_shape=jax.ShapeDtypeStruct((TOK, COLS), BF16),...]
    unnamed x17 -> x1, local copies, waits for them, and re-layouts: 7.54 us -> 1.57 us
where the time goes in v2:
time: 74.6 us; the launch traced here: 74.2 us
  Pallas kernels  72.7 us (97%)
  local copies, waits for them, and re-layouts  1.57 us (2%)
    pallas_call x1, Pallas kernels, local(): pl.pallas_call(kernel, out_shape=jax.ShapeDtypeStruct((TOK, COLS), BF16),...  72.7 us
    unnamed x1, local copies, waits for them, and re-layouts  1.57 us

profile of v2, /device:TPU:16, one launch (start us, length us, event | category | flops | bytes accessed | tf_op | source)
XLA Modules:
  0.0 74.2 jit_solution(4677556706881275248)
XLA Ops:
  0.0 72.7 %shard_map.82 = bf16[128,512]{1,0:T(8,128)(2,1)} custom-call(bf16[128,1024]{1,0:T(8,128)(2,1)} %q_in.1, bf16[128,1024]{1,0:T(8,128)(2,1)} %k_in.1, bf16[128,1024]{1,0:T(8,128)(2,1)} %v_in.1, f32[3,3,1024]{2,1,0:T(4,128)} %sf_hbm.1, f32[16,1024]{1,0:T(8,128)} %bitcast.2, f32[16,1024]{1,0:T(8,128)} %bitcast.3, bf16[128,512]{1,0:T(8,128)(2,1)} %w_in.1, s32[4]{0:T(128)} %rs.1), custom_call_target="tpu_custom_call" | custom-call | tf_op jit(solution)/shard_map/pallas_call | solution.py:540
  72.7 1.6 %copy.10 = bf16[128,512]{1,0:T(8,128)(2,1)} copy(bf16[128,512]{1,0:T(8,128)(2,1)} %shard_map.82) | data formatting | bytes 262144

commit v3 on v2

--- a/solution.py
+++ b/solution.py
@@ -14,6 +14,7 @@
 CH = 1024
 G = CH // 128
 COLS = 512
+WIDE = COLS // 2
 HALF = TOK // 2
 PIECES = 4
 PIECE = TOK // PIECES
@@ -368,7 +369,7 @@
     for cp in to_back:
         cp.start()
     put(ent, z, tile(ebuf, z))
-    for hop in (3, 4, 5):
+    for hop in (3, 4):
         w_hop(hop)
     for cp in to_back:
         cp.wait_recv()
@@ -390,7 +391,7 @@
     state = init
 
     def ablock(yy, cc, h):
-        return abuf.at[yy, cc, pl.ds(h * HALF, HALF), :]
+        return abuf.at[cc, pl.ds(pl.multiple_of(yy * TOK + h * HALF, HALF), HALF), :]
 
     def acopy(yy, h, right, index):
         return pltpu.make_async_remote_copy(
@@ -417,11 +418,13 @@
         state = lax.fori_loop(h * (TOK // 16), (h + 1) * (TOK // 16), correct, state)
         for g in range(G):
             part = gt[pl.ds(h * HALF * G + g, HALF, stride=G), :].astype(BF16)
-            abuf[y, c, h * HALF : (h + 1) * HALF, g * 128 : (g + 1) * 128] = part
+            abuf[c, pl.ds(pl.multiple_of(y * TOK + h * HALF, HALF), HALF), g * 128 : (g + 1) * 128] = part
         if h == 1:
             acopy(y, 1, False, 3).start()
         acopy(y, h, True, h).start()
         sibcopy(0, h).start()
+        if h == 0:
+            w_hop(5)
     acopy(y, 0, False, 2).start()
 
     lhs, rhs, far = ypeer(NY - 1), ypeer(1), ypeer(2)
@@ -438,68 +441,64 @@
     acopy(y, 0, False, 2).wait_recv()
     sibcopy(1, 0).start()
     w_hop(8)
-
-    def product(yy):
-        acc = jnp.dot(abuf[yy, 0], wbuf[0:CH, :], preferred_element_type=F32)
-        return acc + jnp.dot(abuf[yy, 1], wbuf[CH : 2 * CH, :], preferred_element_type=F32)
-
-    def ccopy(d):
+    def product(d, k):
+        rows = pl.ds(pl.multiple_of(ypeer(d) * TOK, TOK), TOK)
+        cols = slice(k * WIDE, (k + 1) * WIDE)
+        acc = jnp.dot(abuf[0, rows, :], wbuf[0:CH, cols], preferred_element_type=F32)
+        acc = acc + jnp.dot(abuf[1, rows, :], wbuf[CH : 2 * CH, cols], preferred_element_type=F32)
+        pbuf[k, rows, :] = acc.astype(BF16)
+
+    def ccopy(d, k):
         return pltpu.make_async_remote_copy(
-            src_ref=pbuf.at[d],
-            dst_ref=qbuf.at[y],
-            send_sem=c_send.at[d],
-            recv_sem=c_recv.at[d],
+            src_ref=pbuf.at[k, pl.ds(pl.multiple_of(ypeer(d) * TOK, TOK), TOK), :],
+            dst_ref=qbuf.at[y, k],
+            send_sem=c_send.at[d, k],
+            recv_sem=c_recv.at[d, k],
             device_id=dev(x, c, ypeer(d), z),
             device_id_type=MESH,
         )
 
-    def xcopy(o, d):
-        return pltpu.make_async_remote_copy(
-            src_ref=qbuf.at[o],
-            dst_ref=rsum.at[x],
-            send_sem=x_send.at[d],
-            recv_sem=x_recv.at[d],
-            device_id=dev(o, c, y, z),
-            device_id_type=MESH,
-        )
-
-    def pass_on(o):
-        for d in range(1, NX):
-            @pl.when(o == xpeer(d))
-            def _():
-                xcopy(xpeer(d), d).start()
-
-        @pl.when(o == x)
-        def _():
-            rsum[x] = qbuf[o]
-
-    def send_product(d):
+    for d in (1, 3):
         for h in range(2):
             sibcopy(d, h).wait_recv()
-        part = product(ypeer(d)).astype(BF16)
-        if d == 0:
-            qbuf[y] = part
-            pass_on(y)
-        else:
-            pbuf[d] = part
-            ccopy(d).start()
-
-    send_product(3)
-    send_product(1)
+        for k in range(2):
+            product(d, k)
+            ccopy(d, k).start()
     acopy(far, 0, True, 4).wait_recv()
     sibcopy(2, 0).start()
     acopy(far, 1, False, 5).wait_recv()
     sibcopy(2, 1).start()
-    send_product(0)
-    send_product(2)
-    for d in (3, 1, 2):
-        ccopy(d).wait_recv()
-        pass_on(ypeer(NY - d))
-    for d in range(1, NX):
-        xcopy(xpeer(d), d).wait_recv()
-    total = rsum[0].astype(F32) + rsum[1].astype(F32) + rsum[2].astype(F32) + rsum[3].astype(F32)
-    out_ref[...] = total.astype(BF16)
-
+
+    def xcopy(o, d, k):
+        return pltpu.make_async_remote_copy(
+            src_ref=qbuf.at[o, k],
+            dst_ref=rsum.at[x, k],
+            send_sem=x_send.at[d, k],
+            recv_sem=x_recv.at[d, k],
+            device_id=dev(o, c, y, z),
+            device_id_type=MESH,
+        )
+
+    def pass_on(o, k):
+        for d in range(1, NX):
+            @pl.when(o == xpeer(d))
+            def _():
+                xcopy(xpeer(d), d, k).start()
+
+        @pl.when(o == x)
+        def _():
+            rsum[x, k] = qbuf[o, k]
+
+    for d in (0, 2):
+        for h in range(2):
+            sibcopy(d, h).wait_recv()
+    for k in range(2):
+        product(2, k)
+        ccopy(2, k).start()
+    for k in range(2):
+        product(0, k)
+        qbuf[y, k] = pbuf[k, pl.ds(pl.multiple_of(y * TOK, TOK), TOK), :]
+        pass_on(y, k)
     @pl.when(x != y)
     def _():
         for k in range(PIECES):
@@ -521,10 +520,23 @@
     for d in range(NY):
         for h in range(2):
             sibcopy(d, h).wait_send()
+
+    for k in range(2):
+        for d in (3, 1, 2):
+            ccopy(d, k).wait_recv()
+            pass_on(ypeer(NY - d), k)
+    for k in range(2):
+        for d in range(1, NX):
+            xcopy(xpeer(d), d, k).wait_recv()
+        total = tree([rsum[i, k].astype(F32) for i in range(NX)])
+        out_ref[:, k * WIDE : (k + 1) * WIDE] = total.astype(BF16)
+
     for d in range(1, NY):
-        ccopy(d).wait_send()
+        for k in range(2):
+            ccopy(d, k).wait_send()
     for d in range(1, NX):
-        xcopy(xpeer(d), d).wait_send()
+        for k in range(2):
+            xcopy(xpeer(d), d, k).wait_send()
 
 
 def local(
@@ -550,14 +562,14 @@
             table, table, table, pltpu.VMEM((G, 128), F32), pltpu.VMEM((NY * G, 128), F32),
             pltpu.VMEM((G, 128), F32), table,
             pltpu.VMEM((NZ * TOK, COLS), BF16),
-            pltpu.VMEM((NY, NC, TOK, CH), BF16),
-            pltpu.VMEM((NY, TOK, COLS), BF16),
-            pltpu.VMEM((NY, TOK, COLS), BF16),
-            pltpu.VMEM((NX, TOK, COLS), BF16),
+            pltpu.VMEM((NC, NY * TOK, CH), BF16),
+            pltpu.VMEM((2, NY * TOK, WIDE), BF16),
+            pltpu.VMEM((NY, 2, TOK, WIDE), BF16),
+            pltpu.VMEM((NX, 2, TOK, WIDE), BF16),
             dma((6,)), dma((3,)), dma((3,)), dma((2, PIECES)), dma((1,)), dma((2, 32)), dma((2, 32)),
             dma((NZ,)), dma((NZ,)), dma((NY,)), dma((NY,)), dma((NZ,)), dma((NZ,)),
             dma((6,)), dma((6,)), dma((NY, 2)), dma((NY, 2)),
-            dma((NY,)), dma((NY,)), dma((NX,)), dma((NX,)),
+            dma((NY, 2)), dma((NY, 2)), dma((NX, 2)), dma((NX, 2)),
         ],
         compiler_params=pltpu.CompilerParams(
             collective_id=0, has_side_effects=True, vmem_limit_bytes=60 * 1024 * 1024

time: 74.6 us -> 73.2 us (0.981)
  the two profiles are of different devices: /device:TPU:16 before, /device:TPU:15 now
where the time goes in v3:
time: 73.2 us; the launch traced here: 73 us
  Pallas kernels  71.5 us (98%)
  local copies, waits for them, and re-layouts  1.57 us (2%)
    pallas_call x1, Pallas kernels, local(): pl.pallas_call(kernel, out_shape=jax.ShapeDtypeStruct((TOK, COLS), BF16),...  71.5 us
    unnamed x1, local copies, waits for them, and re-layouts  1.57 us

profile of v3, /device:TPU:15, one launch (start us, length us, event | category | flops | bytes accessed | tf_op | source)
XLA Modules:
  0.0 73.0 jit_solution(6022333949946643919)
XLA Ops:
  0.0 71.5 %shard_map.82 = bf16[128,512]{1,0:T(8,128)(2,1)} custom-call(bf16[128,1024]{1,0:T(8,128)(2,1)} %q_in.1, bf16[128,1024]{1,0:T(8,128)(2,1)} %k_in.1, bf16[128,1024]{1,0:T(8,128)(2,1)} %v_in.1, f32[3,3,1024]{2,1,0:T(4,128)} %sf_hbm.1, f32[16,1024]{1,0:T(8,128)} %bitcast.2, f32[16,1024]{1,0:T(8,128)} %bitcast.3, bf16[128,512]{1,0:T(8,128)(2,1)} %w_in.1, s32[4]{0:T(128)} %rs.1), custom_call_target="tpu_custom_call" | custom-call | tf_op jit(solution)/shard_map/pallas_call | solution.py:552
  71.5 1.6 %copy.10 = bf16[128,512]{1,0:T(8,128)(2,1)} copy(bf16[128,512]{1,0:T(8,128)(2,1)} %shard_map.82) | data formatting | bytes 262144

commit v4 on v3

--- a/solution.py
+++ b/solution.py
@@ -458,16 +458,20 @@
             device_id_type=MESH,
         )
 
-    for d in (1, 3):
-        for h in range(2):
-            sibcopy(d, h).wait_recv()
-        for k in range(2):
-            product(d, k)
-            ccopy(d, k).start()
+    for h in range(2):
+        sibcopy(1, h).wait_recv()
+    for k in range(2):
+        product(1, k)
+        ccopy(1, k).start()
     acopy(far, 0, True, 4).wait_recv()
     sibcopy(2, 0).start()
     acopy(far, 1, False, 5).wait_recv()
     sibcopy(2, 1).start()
+    for h in range(2):
+        sibcopy(3, h).wait_recv()
+    for k in range(2):
+        product(3, k)
+        ccopy(3, k).start()
 
     def xcopy(o, d, k):
         return pltpu.make_async_remote_copy(

time: 73.2 us -> 72.5 us (level)
  the two profiles are of different devices: /device:TPU:15 before, /device:TPU:5 now
where the time goes in v4:
time: 72.5 us; the launch traced here: 72.3 us
  Pallas kernels  70.8 us (98%)
  local copies, waits for them, and re-layouts  1.57 us (2%)
    pallas_call x1, Pallas kernels, local(): pl.pallas_call(kernel, out_shape=jax.ShapeDtypeStruct((TOK, COLS), BF16),...  70.8 us
    unnamed x1, local copies, waits for them, and re-layouts  1.57 us

profile of v4, /device:TPU:5, one launch (start us, length us, event | category | flops | bytes accessed | tf_op | source)
XLA Modules:
  0.0 72.3 jit_solution(8512813536396332952)
XLA Ops:
  0.0 70.8 %shard_map.82 = bf16[128,512]{1,0:T(8,128)(2,1)} custom-call(bf16[128,1024]{1,0:T(8,128)(2,1)} %q_in.1, bf16[128,1024]{1,0:T(8,128)(2,1)} %k_in.1, bf16[128,1024]{1,0:T(8,128)(2,1)} %v_in.1, f32[3,3,1024]{2,1,0:T(4,128)} %sf_hbm.1, f32[16,1024]{1,0:T(8,128)} %bitcast.2, f32[16,1024]{1,0:T(8,128)} %bitcast.3, bf16[128,512]{1,0:T(8,128)(2,1)} %w_in.1, s32[4]{0:T(128)} %rs.1), custom_call_target="tpu_custom_call" | custom-call | tf_op jit(solution)/shard_map/pallas_call | solution.py:556
  70.8 1.6 %copy.10 = bf16[128,512]{1,0:T(8,128)(2,1)} copy(bf16[128,512]{1,0:T(8,128)(2,1)} %shard_map.82) | data formatting | bytes 262144
